TPU v7x, 32 devices: a whole 2x2x4 slice. The times are simulated.
32 devices in a mesh: groups: 2 (over y), atoms: 4 (over z), chan: 2 (over x), sub: 2 (over core).
Axes of the slice: x: 2, y: 2, z: 4, core: 2. Of those that a mesh axis runs over, the one named last changes fastest.
Arguments:
- cotangent: bfloat16 [29, 64, 12288], P(None, ('chan', 'sub'), ('groups', 'atoms')), parts along dimension 2, may hold values from -6 to 6
- wigner: bfloat16 [235, 12288], P(None, ('groups', 'atoms')), parts along dimension 1, may hold values from -2.390625 to 2.390625
- sender_ids: int32 [12288], P(('groups', 'atoms')), parts along dimension 0, may hold values from 0 to 63, as said below
- receiver_slots: int32 [12288], P(('groups', 'atoms')), parts along dimension 0, may hold values from 0 to 31
- destinations: int32 [96], P(('groups', 'atoms')), parts along dimension 0, may hold values from 0 to 3, as said below
- live_counts: int32 [96], P(('groups', 'atoms')), parts along dimension 0, may hold values from 32 to 128, as said below
- receiver_lists: int32 [96, 32], P(('groups', 'atoms')), parts along dimension 0, may hold values from 0 to 63, as said below
- weight_zero: bfloat16 [7, 2, 128, 7, 64], P(None, None, ('chan', 'sub')), may hold values from -0.125 to 0.125
- real_one: bfloat16 [6, 2, 128, 6, 64], P(None, None, ('chan', 'sub')), may hold values from -0.15625 to 0.15625
- imag_one: bfloat16 [6, 2, 128, 6, 64], P(None, None, ('chan', 'sub')), may hold values from -0.15625 to 0.15625
- real_two: bfloat16 [5, 2, 128, 5, 64], P(None, None, ('chan', 'sub')), may hold values from -0.15625 to 0.15625
- imag_two: bfloat16 [5, 2, 128, 5, 64], P(None, None, ('chan', 'sub')), may hold values from -0.15625 to 0.15625
- to_grid: bfloat16 [196, 49], replicated, may hold values from -0.875 to 0.875
- from_grid: bfloat16 [49, 196], replicated, may hold values from -0.4375 to 0.4375
- pre_act: bfloat16 [49, 128, 512], P(None, ('chan', 'sub'), ('groups', 'atoms')), parts along dimension 2, may hold values from -6 to 6
Outputs:
- grad_pre: bfloat16 [49, 128, 512], P(None, ('chan', 'sub'), ('groups', 'atoms')), parts along dimension 2
There are 2 independent parts, one for each index of `groups`. A program takes and returns all parts, laid end to end along the dimension named above; an argument that names none is the same for every part. Nothing has to cross between parts.
Inputs may be any that keep to these rules, and one draw needn't show every extreme that they name: `sender_ids`: within one shard's edges the senders never fall. `destinations`: the blocks of one shard name each shard at most 3 times, and some shard exactly that often. `live_counts`: live edges stand at the head of a block; the rest is padding. Some block of every shard is full. `receiver_lists`: each block lists 32 distinct atoms of its destination shard.
All inputs are finite; a program needn't handle non-finite values.
Results may differ from a plain program's by a relative error of at most 0.0068.
Values may be sent and summed in bfloat16 or wider, within the bound.
A program may use at most 128 MiB of HBM per device.

v0:
```python
import jax
import jax.numpy as jnp
from jax import lax
from jax.sharding import PartitionSpec as P


def contract(weight, piece):
    return jnp.einsum("ahcbq,bqe->ahce", weight, piece, preferred_element_type=jnp.float32)


def so2_transpose(piece, weights):
    weight_zero, real_one, imag_one, real_two, imag_two = weights
    zero_rows = contract(weight_zero, piece[0:7])
    plus_one = contract(real_one, piece[7:13]) + contract(imag_one, piece[13:19])
    minus_one = contract(real_one, piece[13:19]) - contract(imag_one, piece[7:13])
    plus_two = contract(real_two, piece[19:24]) + contract(imag_two, piece[24:29])
    minus_two = contract(real_two, piece[24:29]) - contract(imag_two, piece[19:24])
    return (zero_rows, plus_one, minus_one, plus_two, minus_two)


def rotate_back(grad_parts, wigner):
    zero_rows, plus_one, minus_one, plus_two, minus_two = grad_parts
    pieces_out = []
    offset = 0
    for degree in range(7):
        m_reach = min(degree, 2)
        edge_rows = []
        if m_reach >= 2:
            edge_rows.append(minus_two[degree - 2])
        if m_reach >= 1:
            edge_rows.append(minus_one[degree - 1])
        edge_rows.append(zero_rows[degree])
        if m_reach >= 1:
            edge_rows.append(plus_one[degree - 1])
        if m_reach >= 2:
            edge_rows.append(plus_two[degree - 2])
        span_width = 2 * degree + 1
        summed = jnp.zeros((span_width,) + edge_rows[0].shape, jnp.float32)
        for position, edge_row in enumerate(edge_rows):
            start_row = offset + position * span_width
            coeffs = wigner[start_row : start_row + span_width].astype(jnp.float32)
            summed = summed + coeffs[:, None, None, :] * edge_row[None]
        offset = offset + len(edge_rows) * span_width
        pieces_out.append(summed.astype(jnp.bfloat16))
    return jnp.concatenate(pieces_out, axis=0)


def sphere_backward(to_grid, from_grid, pre_flat, atom_grad):
    grid_pre = jnp.dot(to_grid, pre_flat, preferred_element_type=jnp.float32)
    grid_grad = lax.dot_general(
        from_grid, atom_grad, (((0,), (0,)), ((), ())), preferred_element_type=jnp.float32
    )
    sigmoid_of = jax.nn.sigmoid(grid_pre)
    grid_term = (sigmoid_of * (1.0 + grid_pre * (1.0 - sigmoid_of)) * grid_grad).astype(
        jnp.bfloat16
    )
    return lax.dot_general(
        to_grid, grid_term, (((0,), (0,)), ((), ())), preferred_element_type=jnp.float32
    ).astype(jnp.bfloat16)


def add_parts(right_parts):
    return tuple((right_one for right_one in right_parts))


def per_device(
    cotangent,
    wigner,
    sender_ids,
    receiver_slots,
    destinations,
    live_counts,
    receiver_lists,
    weight_zero,
    real_one,
    imag_one,
    real_two,
    imag_two,
    to_grid,
    from_grid,
    pre_act,
):
    edge_total = cotangent.shape[2]
    block_count = destinations.shape[0]
    block_width = edge_total // block_count
    coef_rows = pre_act.shape[0]
    chan_share = pre_act.shape[1]
    atom_share = pre_act.shape[2]
    slot_width = receiver_lists.shape[1]
    shard_count = lax.axis_size("atoms")
    per_dest = (block_count + shard_count - 1) // shard_count
    slot_total = shard_count * per_dest
    weights = (weight_zero, real_one, imag_one, real_two, imag_two)
    weight_cols = tuple((weight for weight in weights))
    grad_parts = add_parts(
        so2_transpose(lax.all_gather(cotangent, ("chan", "sub"), axis=1, tiled=True), weight_cols)
    )
    rotated = rotate_back(grad_parts, wigner)
    live_edge = (
        lax.broadcasted_iota(jnp.int32, (block_count, block_width), 1) < live_counts[:, None]
    )
    live_flat = live_edge.reshape(edge_total)
    atom_axis = jnp.arange(atom_share, dtype=jnp.int32)
    sender_rows = rotated[:, 0].reshape(coef_rows * chan_share, edge_total)
    sender_hot = ((sender_ids[:, None] == atom_axis[None, :]) & live_flat[:, None]).astype(
        jnp.bfloat16
    )
    sender_sum = jnp.dot(sender_rows, sender_hot, preferred_element_type=jnp.float32)
    receiver_rows = rotated[:, 1].reshape(coef_rows * chan_share, block_count, block_width)
    slot_grid = receiver_slots.reshape(block_count, block_width)
    slot_axis = jnp.arange(slot_width, dtype=jnp.int32)
    block_axis = jnp.arange(block_count, dtype=jnp.int32)
    same_dest = destinations[:, None] == destinations[None, :]
    earlier = jnp.sum(same_dest & (block_axis[:, None] > block_axis[None, :]), axis=1)
    placement = destinations * per_dest + earlier
    place_hot = placement[:, None] == jnp.arange(slot_total, dtype=jnp.int32)[None, :]
    slot_hot = ((slot_grid[:, :, None] == slot_axis[None, None, :]) & live_edge[:, :, None]).astype(
        jnp.bfloat16
    )
    block_sums = jnp.einsum(
        "kbw,bwr->bkr", receiver_rows, slot_hot, preferred_element_type=jnp.float32
    ).astype(jnp.bfloat16)
    send_sums = jnp.einsum(
        "bs,bkr->ksr",
        place_hot.astype(jnp.bfloat16),
        block_sums,
        preferred_element_type=jnp.float32,
    ).astype(jnp.bfloat16)
    list_send = (
        jnp.sum(place_hot.astype(jnp.int32)[:, :, None] * (receiver_lists[:, None, :] + 1), axis=0)
        - 1
    )
    list_wire = list_send.astype(jnp.float32).astype(jnp.bfloat16)[None]
    got_sums, got_lists = (
        lax.all_to_all(send_sums, "atoms", split_axis=1, concat_axis=1, tiled=True),
        lax.all_to_all(list_wire, "atoms", split_axis=1, concat_axis=1, tiled=True),
    )
    got_ids = got_lists[0].astype(jnp.float32).astype(jnp.int32).reshape(slot_total * slot_width)
    got_hot = (got_ids[:, None] == atom_axis[None, :]).astype(jnp.bfloat16)
    receiver_sum = jnp.dot(
        got_sums.reshape(coef_rows * chan_share, slot_total * slot_width),
        got_hot,
        preferred_element_type=jnp.float32,
    )
    atom_grad = (
        (sender_sum + receiver_sum).astype(jnp.bfloat16).reshape(coef_rows, chan_share * atom_share)
    )
    result = sphere_backward(
        to_grid, from_grid, pre_act.reshape(coef_rows, chan_share * atom_share), atom_grad
    )
    return result.reshape(coef_rows, chan_share, atom_share)


def solution(mesh):
    in_specs = (
        P(None, ("chan", "sub"), ("groups", "atoms")),
        P(None, ("groups", "atoms")),
        P(("groups", "atoms")),
        P(("groups", "atoms")),
        P(("groups", "atoms")),
        P(("groups", "atoms")),
        P(("groups", "atoms"), None),
        P(None, None, ("chan", "sub"), None, None),
        P(None, None, ("chan", "sub"), None, None),
        P(None, None, ("chan", "sub"), None, None),
        P(None, None, ("chan", "sub"), None, None),
        P(None, None, ("chan", "sub"), None, None),
        P(),
        P(),
        P(None, ("chan", "sub"), ("groups", "atoms")),
    )
    out_specs = P(None, ("chan", "sub"), ("groups", "atoms"))
    return jax.shard_map(
        per_device, mesh=mesh, in_specs=in_specs, out_specs=out_specs, check_vma=False
    )
```

profile of v0, /device:TPU:0, one launch (start us, length us, event | category | flops | bytes accessed | tf_op | source)
XLA Modules:
  0.0 153.7 jit_solution(2751970899024850034)
XLA Ops:
  6.5 0.7 all-gather.2.cloned.1.call-update
  7.3 0.9 convert_reduce_fusion
  8.2 0.7 multiply_add_fusion
  8.8 0.5 copy-done.18
  9.4 0.7 broadcast_add_fusion
  10.2 0.6 copy.39
  10.8 6.3 %all-to-all-start.1 = ((bf16[1,12,32]{2,0,1:T(2,128)(2,1)}), bf16[1,12,32]{2,0,1:T(2,128)(2,1)}, u32[]{:S(2)}, u32[]{:S(2)}) async-start(bf16[1,12,32]{2,0,1:T(2,128)(2,1)} %copy.39), calls=%async_computation.1 | async-start | bytes 12288 | tf_op jit(solution)/shard_map/all_to_all | solution.py:136
  17.1 0.8 convert_reduce_fusion.1
  17.9 1.3 iota_compare_fusion.6
  19.2 1.5 slice_convert_fusion.27
  20.7 1.7 %slice_convert_fusion.24 = (f32[5,1536]{1,0:T(8,128)}, f32[5,1536]{1,0:T(8,128)}, f32[5,1536]{1,0:T(8,128)}, f32[5,1536]{1,0:T(8,128)}, f32[5,1536]{1,0:T(8,128)}) fusion(bf16[235,1536]{1,0:T(8,128)(2,1)} %param.16), kind=kLoop, calls=%fused_computation.112 | loop fusion | flops 38400 | bytes 230400 | tf_op jit(solution)/shard_map/convert_element_type | solution.py:41
  22.4 1.6 %slice_convert_fusion.19 = (f32[7,1536]{1,0:T(8,128)S(1)}, f32[7,1536]{1,0:T(8,128)S(1)}, f32[7,1536]{1,0:T(8,128)}, f32[7,1536]{1,0:T(8,128)}, f32[7,1536]{1,0:T(8,128)}) fusion(bf16[235,1536]{1,0:T(8,128)(2,1)} %param.16), kind=kLoop, calls=%fused_computation.107 | loop fusion | flops 53760 | bytes 322560 | tf_op jit(solution)/shard_map/convert_element_type | solution.py:41
  23.9 1.1 slice_convert_fusion.14
  25.2 29.5 %all-gather.2.cloned.1.call-done = bf16[29,64,1536]{2,1,0:T(8,128)(2,1)} async-done(((bf16[29,16,1536]{2,1,0:T(8,128)(2,1)}), bf16[29,64,1536]{2,1,0:T(8,128)(2,1)}) %all-gather.2.cloned.1.call-update) | async-done | bytes 5701648 | tf_op jit(solution)/shard_map/all_gather | solution.py:96
  54.7 2.2 %convolution_bitcast_fusion.7 = f32[5,2,32,1536]{3,2,1,0:T(8,128)S(1)} fusion(bf16[5,2,32,5,64]{4,2,3,1,0:T(8,128)(2,1)} %param.26, bf16[29,64,1536]{2,1,0:T(8,128)(2,1)} %all-gather.2.cloned.1.call-done), kind=kOutput, calls=%fused_computation.15 | convolution fusion | flops 314572800 | bytes 3358720 | tf_op jit(solution)/shard_map/ahcbq,bqe->ahce/dot_general | solution.py:8
  56.9 2.0 %fusion.4 = f32[5,2,32,1536]{3,2,1,0:T(8,128)S(1)} fusion(f32[5,2,32,1536]{3,2,1,0:T(8,128)S(1)} %convolution_bitcast_fusion.7, bf16[5,2,32,5,64]{4,2,3,1,0:T(8,128)(2,1)S(1)} %copy-done.2, bf16[29,64,1536]{2,1,0:T(8,128)(2,1)} %all-gather.2.cloned.1.call-done), kind=kOutput, calls=%fused_computation.17 | convolution fusion | flops 315064320 | bytes 5120000 | tf_op jit(solution)/shard_map/ahcbq,bqe->ahce/dot_general | solution.py:8
  59.1 0.9 copy-done.21
  60.0 0.8 convolution_bitcast_fusion.1
  60.9 0.9 convolution_bitcast_fusion
  61.9 0.8 fusion.3
  62.7 0.5 slice_bitcast_fusion.15
  63.3 0.7 fusion.29
  64.0 0.7 convolution_bitcast_fusion.5
  64.7 0.8 convolution_bitcast_fusion.3
  65.5 0.7 fusion.5
  66.3 0.8 fusion.2
  67.2 0.4 slice_bitcast_fusion.14
  67.8 1.1 fusion.24
  68.9 1.6 %fusion.19 = bf16[49,2,32,1536]{3,2,0,1:T(8,128)(2,1)} fusion(bf16[49,2,32,1536]{3,2,0,1:T(8,128)(2,1)} %fusion.24, f32[2,32,1536]{2,1,0:T(8,128)S(1)} %get-tuple-element.34, f32[5,1536]{1,0:T(8,128)S(1)} %copy-done.9, f32[2,32,1536]{2,1,0:T(8,128)S(1)} %get-tuple-element.23, f32[5,1536]{1,0:T(8,128)S(1)} %copy-done.10, ...), kind=kLoop, calls=%fused_computation.39 | loop fusion | flops 4915200 | bytes 3102720
  70.5 2.0 %fusion.18 = bf16[49,2,32,1536]{3,2,0,1:T(8,128)(2,1)} fusion(bf16[49,2,32,1536]{3,2,0,1:T(8,128)(2,1)} %fusion.19, f32[2,32,1536]{2,1,0:T(8,128)S(1)} %get-tuple-element.33, f32[7,1536]{1,0:T(8,128)S(1)} %get-tuple-element.51, f32[2,32,1536]{2,1,0:T(8,128)S(1)} %get-tuple-element.22, f32[7,1536]{1,0:T(8,128)S(1)} %copy-done.5, ...), kind=kLoop, calls=%fused_computation.34 | loop fusion | flops 6881280 | bytes 3557376
  72.5 2.3 %fusion.16 = bf16[49,2,32,1536]{3,2,0,1:T(8,128)(2,1)} fusion(bf16[49,2,32,1536]{3,2,0,1:T(8,128)(2,1)} %fusion.18, f32[2,32,1536]{2,1,0:T(8,128)S(1)} %get-tuple-element.32, f32[9,1536]{1,0:T(8,128)S(1)} %get-tuple-element.46, f32[2,32,1536]{2,1,0:T(8,128)S(1)} %get-tuple-element.21, f32[9,1536]{1,0:T(8,128)S(1)} %get-tuple-element.47, ...), kind=kLoop, calls=%fused_computation.32 | loop fusion | flops 8847360 | bytes 4012032
  74.8 2.8 %fusion.15 = bf16[49,2,32,1536]{3,2,0,1:T(8,128)(2,1)} fusion(bf16[49,2,32,1536]{3,2,0,1:T(8,128)(2,1)} %fusion.16, f32[2,32,1536]{2,1,0:T(8,128)S(1)} %get-tuple-element.31, f32[11,1536]{1,0:T(8,128)S(1)} %get-tuple-element.41, f32[2,32,1536]{2,1,0:T(8,128)S(1)} %get-tuple-element.20, f32[11,1536]{1,0:T(8,128)S(1)} %get-tuple-element.42, ...), kind=kLoop, calls=%fused_computation.30 | loop fusion | flops 10813440 | bytes 4466688
  77.6 2.9 %fusion.11 = bf16[49,2,32,1536]{3,2,0,1:T(8,128)(2,1)} fusion(bf16[49,2,32,1536]{3,2,0,1:T(8,128)(2,1)} %fusion.15, f32[2,32,1536]{2,1,0:T(8,128)S(1)} %get-tuple-element.30, f32[13,1536]{1,0:T(8,128)S(1)} %get-tuple-element.38, f32[2,32,1536]{2,1,0:T(8,128)S(1)} %get-tuple-element.19, f32[13,1536]{1,0:T(8,128)S(1)} %get-tuple-element.39, ...), kind=kLoop, calls=%fused_computation.24 | loop fusion | flops 12779520 | bytes 4921344 | tf_op jit(solution)/shard_map/concatenate | solution.py:45
  80.4 8.8 %fusion.43 = (bf16[49,1,32,1536]{3,2,0,1:T(8,128)(2,1)}, bf16[49,1,32,1536]{3,2,0,1:T(8,128)(2,1)}) fusion(bf16[49,2,32,1536]{3,2,0,1:T(8,128)(2,1)} %fusion.11), kind=kLoop, calls=%fused_computation.132 | loop fusion | bytes 19267584 | tf_op jit(solution)/shard_map/slice | solution.py:109
  89.3 9.8 %reshape_squeeze.7 = bf16[1568,12,128]{2,1,0:T(8,128)(2,1)} reshape(bf16[49,1,32,1536]{3,2,0,1:T(8,128)(2,1)} %get-tuple-element.5) | data formatting | bytes 9633792 | tf_op jit(solution)/shard_map/reshape;squeeze | solution.py:109
  99.0 5.5 %fusion.6 = bf16[12,1568,32]{1,2,0:T(8,128)(2,1)S(1)} fusion(bf16[1568,12,128]{2,1,0:T(8,128)(2,1)} %reshape_squeeze.7, s32[12,128]{1,0:T(8,128)S(1)} %bitcast.170, pred[12,128]{1,0:T(8,128)(4,1)S(1)} %copy-done.20), kind=kOutput, calls=%fused_computation.19 | convolution fusion | flops 154841088 | bytes 6028800 | tf_op jit(solution)/shard_map/kbw,bwr->bkr/dot_general | solution.py:120
  104.6 0.6 fusion.9
  105.2 1.3 copy.37
  106.5 4.7 %all-to-all-start = ((bf16[1568,12,32]{0,2,1:T(8,128)(2,1)}), bf16[1568,12,32]{0,2,1:T(8,128)(2,1)S(1)}, u32[]{:S(2)}, u32[]{:S(2)}) async-start(bf16[1568,12,32]{0,2,1:T(8,128)(2,1)} %copy.37), calls=%async_computation | async-start | bytes 2555904 | tf_op jit(solution)/shard_map/all_to_all | solution.py:135
  111.2 0.3 reshape.128
  111.6 1.6 %fusion.44 = f32[196,2048]{1,0:T(8,128)} fusion(bf16[196,49]{0,1:T(8,128)(2,1)S(1)} %copy-done.15, bf16[49,2048]{1,0:T(8,128)(2,1)S(1)} %reshape.128), kind=kOutput, calls=%fused_computation.133 | convolution fusion | flops 39337984 | bytes 1825544 | tf_op jit(solution)/shard_map/dot_general | solution.py:49
  113.2 0.7 convert_reduce_fusion.2
  114.0 3.8 %fusion.22 = f32[1568,64]{0,1:T(8,128)S(1)} fusion(bf16[1568,1536]{1,0:T(8,128)(2,1)} %bitcast.166, s32[1536]{0:T(1024)S(1)} %copy-done.16, pred[1536]{0:T(1024)(128)(4,1)S(1)} %copy-done.17), kind=kOutput, calls=%fused_computation.45 | convolution fusion | flops 308477952 | bytes 5225984 | tf_op jit(solution)/shard_map/dot_general | solution.py:108
  117.8 24.5 %all-to-all-done = bf16[1568,12,32]{0,2,1:T(8,128)(2,1)S(1)} async-done(((bf16[1568,12,32]{0,2,1:T(8,128)(2,1)}), bf16[1568,12,32]{0,2,1:T(8,128)(2,1)S(1)}, u32[]{:S(2)}, u32[]{:S(2)}) %all-to-all-start) | async-done | bytes 1204256 | tf_op jit(solution)/shard_map/all_to_all | solution.py:135
  142.3 0.5 fusion.13
  143.0 0.3 reshape.130
  143.4 2.3 %fusion.14 = bf16[49,2048]{1,0:T(8,128)(2,1)S(1)} fusion(bf16[196,49]{0,1:T(8,128)(2,1)S(1)} %copy-done.15, bf16[49,2048]{1,0:T(8,128)(2,1)S(1)} %reshape.130, bf16[49,196]{1,0:T(8,128)(2,1)S(1)} %copy-done.24, f32[196,2048]{1,0:T(8,128)} %fusion.44), kind=kOutput, calls=%fused_computation.29 | convolution fusion | flops 82388992 | bytes 2045456 | tf_op jit(solution)/shard_map/dot_general | solution.py:57
  145.7 1.1 reshape.131
  (66 shorter events, 1.2 us)
Async XLA Ops:
  6.5 54.3 %copy-start = (bf16[7,2,32,7,64]{4,2,3,1,0:T(8,128)(2,1)S(1)}, bf16[7,2,32,7,64]{4,2,3,1,0:T(8,128)(2,1)}, u32[]{:S(2)}) copy-start(bf16[7,2,32,7,64]{4,2,3,1,0:T(8,128)(2,1)} %param.22) | copy-start | bytes 1204228
  6.5 18.5 %copy-start.3 = (bf16[235,1536]{1,0:T(8,128)(2,1)S(1)}, bf16[235,1536]{1,0:T(8,128)(2,1)}, u32[]{:S(2)}) copy-start(bf16[235,1536]{1,0:T(8,128)(2,1)} %param.16) | copy-start | bytes 2165764
  6.5 48.1 %all-gather.2.cloned.1.call-start = ((), (), s32[]{:S(2)}) async-start(), calls=%async_computation.2 | async-start | bytes 7127040 | tf_op jit(solution)/shard_map/all_gather | solution.py:96
  8.8 0.5 copy-start.18
  10.8 95.7 %all-to-all-start.1 = ((bf16[1,12,32]{2,0,1:T(2,128)(2,1)}), bf16[1,12,32]{2,0,1:T(2,128)(2,1)}, u32[]{:S(2)}, u32[]{:S(2)}) async-start(bf16[1,12,32]{2,0,1:T(2,128)(2,1)} %copy.39), calls=%async_computation.1 | async-start | bytes 12288 | tf_op jit(solution)/shard_map/all_to_all | solution.py:136
  25.0 31.8 %copy-start.2 = (bf16[5,2,32,5,64]{4,2,3,1,0:T(8,128)(2,1)S(1)}, bf16[5,2,32,5,64]{4,2,3,1,0:T(8,128)(2,1)}, u32[]{:S(2)}) copy-start(bf16[5,2,32,5,64]{4,2,3,1,0:T(8,128)(2,1)} %param.25) | copy-start | bytes 614404
  54.7 4.4 %slice-start = ((s8[5701632]{0:T(1024)(128)(4,1)}), s8[4194304]{0:T(1024)(128)(4,1)S(1)}, s32[]{:S(2)}) async-start(s8[5701632]{0:T(1024)(128)(4,1)} %bitcast.168), calls=%async_computation.3 | async-start | bytes 8388608
  56.9 2.2 %slice-start.1 = ((s8[5701632]{0:T(1024)(128)(4,1)}), s8[1507328]{0:T(1024)(128)(4,1)S(1)}, s32[]{:S(2)}) async-start(s8[5701632]{0:T(1024)(128)(4,1)} %bitcast.168), calls=%async_computation.4 | async-start | bytes 3014656
  58.9 1.1 copy-start.21
  60.8 1.1 copy-start.22
  62.7 1.3 copy-start.23
  67.1 0.7 copy-start.13
  67.1 0.7 copy-start.14
  67.1 1.8 %copy-start.8 = (f32[5,1536]{1,0:T(8,128)S(1)}, f32[5,1536]{1,0:T(8,128)}, u32[]{:S(2)}) copy-start(f32[5,1536]{1,0:T(8,128)} %get-tuple-element.55) | copy-start | bytes 92164
  67.1 1.8 %copy-start.9 = (f32[5,1536]{1,0:T(8,128)S(1)}, f32[5,1536]{1,0:T(8,128)}, u32[]{:S(2)}) copy-start(f32[5,1536]{1,0:T(8,128)} %get-tuple-element.56) | copy-start | bytes 92164
  67.1 1.8 %copy-start.10 = (f32[5,1536]{1,0:T(8,128)S(1)}, f32[5,1536]{1,0:T(8,128)}, u32[]{:S(2)}) copy-start(f32[5,1536]{1,0:T(8,128)} %get-tuple-element.57) | copy-start | bytes 92164
  67.1 1.8 %copy-start.11 = (f32[5,1536]{1,0:T(8,128)S(1)}, f32[5,1536]{1,0:T(8,128)}, u32[]{:S(2)}) copy-start(f32[5,1536]{1,0:T(8,128)} %get-tuple-element.58) | copy-start | bytes 92164
  67.1 1.8 %copy-start.12 = (f32[5,1536]{1,0:T(8,128)S(1)}, f32[5,1536]{1,0:T(8,128)}, u32[]{:S(2)}) copy-start(f32[5,1536]{1,0:T(8,128)} %get-tuple-element.59) | copy-start | bytes 92164
  67.6 2.9 %copy-start.5 = (f32[7,1536]{1,0:T(8,128)S(1)}, f32[7,1536]{1,0:T(8,128)}, u32[]{:S(2)}) copy-start(f32[7,1536]{1,0:T(8,128)} %get-tuple-element.52) | copy-start | bytes 129028
  67.6 2.9 %copy-start.6 = (f32[7,1536]{1,0:T(8,128)S(1)}, f32[7,1536]{1,0:T(8,128)}, u32[]{:S(2)}) copy-start(f32[7,1536]{1,0:T(8,128)} %get-tuple-element.53) | copy-start | bytes 129028
  67.6 2.9 %copy-start.7 = (f32[7,1536]{1,0:T(8,128)S(1)}, f32[7,1536]{1,0:T(8,128)}, u32[]{:S(2)}) copy-start(f32[7,1536]{1,0:T(8,128)} %get-tuple-element.54) | copy-start | bytes 129028
  89.3 9.8 %copy-start.20 = (pred[12,128]{1,0:T(8,128)(4,1)S(1)}, pred[12,128]{1,0:T(8,128)(4,1)}, u32[]{:S(2)}) copy-start(pred[12,128]{1,0:T(8,128)(4,1)} %get-tuple-element.63) | copy-start | bytes 4612
  89.3 9.8 %copy-start.25 = (s32[1536]{0:T(1024)S(1)}, s32[1536]{0:T(1024)}, u32[]{:S(2)}) copy-start(s32[1536]{0:T(1024)} %param.18) | copy-start | bytes 18436
  99.0 5.5 %copy-start.19 = (s32[12]{0:T(128)S(1)}, s32[12]{0:T(128)}, u32[]{:S(2)}) copy-start(s32[12]{0:T(128)} %copy-done.18) | copy-start | bytes 148
  105.2 6.0 %copy-start.4 = (bf16[49,32,64]{2,1,0:T(8,128)(2,1)S(1)}, bf16[49,32,64]{2,1,0:T(8,128)(2,1)}, u32[]{:S(2)}) copy-start(bf16[49,32,64]{2,1,0:T(8,128)(2,1)} %param.29) | copy-start | bytes 602116
  105.2 6.4 %copy-start.15 = (bf16[196,49]{0,1:T(8,128)(2,1)S(1)}, bf16[196,49]{0,1:T(8,128)(2,1)}, u32[]{:S(2)}) copy-start(bf16[196,49]{0,1:T(8,128)(2,1)} %param.27) | copy-start | bytes 57628
  106.5 7.5 %copy-start.16 = (s32[1536]{0:T(1024)S(1)}, s32[1536]{0:T(1024)}, u32[]{:S(2)}) copy-start(s32[1536]{0:T(1024)} %param.17) | copy-start | bytes 18436
  106.5 7.5 %copy-start.17 = (pred[1536]{0:T(1024)(128)(4,1)S(1)}, pred[1536]{0:T(1024)(128)(4,1)}, u32[]{:S(2)}) copy-start(pred[1536]{0:T(1024)(128)(4,1)} %get-tuple-element.64) | copy-start | bytes 4612
  106.5 35.8 %all-to-all-start = ((bf16[1568,12,32]{0,2,1:T(8,128)(2,1)}), bf16[1568,12,32]{0,2,1:T(8,128)(2,1)S(1)}, u32[]{:S(2)}, u32[]{:S(2)}) async-start(bf16[1568,12,32]{0,2,1:T(8,128)(2,1)} %copy.37), calls=%async_computation | async-start | bytes 2555904 | tf_op jit(solution)/shard_map/all_to_all | solution.py:135
  117.8 25.6 %copy-start.24 = (bf16[49,196]{1,0:T(8,128)(2,1)S(1)}, bf16[49,196]{1,0:T(8,128)(2,1)}, u32[]{:S(2)}) copy-start(bf16[49,196]{1,0:T(8,128)(2,1)} %param.28) | copy-start | bytes 57628
  143.0 3.8 %copy-start.1 = (bf16[7,2,32,7,64]{4,2,3,1,0:T(8,128)(2,1)S(1)}, bf16[7,2,32,7,64]{4,2,3,1,0:T(8,128)(2,1)}, u32[]{:S(2)}) copy-start(bf16[7,2,32,7,64]{4,2,3,1,0:T(8,128)(2,1)} %param.22) | copy-start | bytes 1204228
Sparse Core Ops, SparseCore 0:
  8.9 45.7 all-gather.1
where the time goes:
time: 155 us; the launch traced here: 154 us
  waiting for transfers between devices  54.7 us (35%)
  local copies, waits for them, and re-layouts  25.6 us (17%)
  other arithmetic  24.4 us (16%)
  matrix products  24.1 us (16%)
  between operations  13.8 us (9%)
  starting transfers between devices  11.1 us (7%)
    all_gather x1, waiting for transfers between devices, per_device(): lax.all_gather(cotangent, ('chan', 'sub'), axis=1, tiled=True)  29.5 us
    all_to_all x1, waiting for transfers between devices, per_device(): lax.all_to_all(send_sums, 'atoms', split_axis=1, concat_axis=1, tiled=True)  24.5 us
    unnamed x7, other arithmetic  10.4 us
    dot_general x9, matrix products, contract(): jnp.einsum('ahcbq,bqe->ahce', weight, piece, preferred_element_type=jnp.f...  9.81 us
    another operation x1, local copies, waits for them, and re-layouts, per_device(): rotated[:, 1].reshape(coef_rows * chan_share, block_count, block_width)  9.78 us
    slice x1, local copies, waits for them, and re-layouts, per_device(): rotated[:, 1].reshape(coef_rows * chan_share, block_count, block_width)  8.81 us
    all_to_all x1, starting transfers between devices, per_device(): lax.all_to_all(list_wire, 'atoms', split_axis=1, concat_axis=1, tiled=True)  6.32 us
    convert_element_type x6, other arithmetic, rotate_back(): coeffs = wigner[start_row:start_row + span_width].astype(jnp.float32)  5.89 us
  transfers between devices with their start and end apart: 3, of which 2 were waited for; matrix products, arithmetic and copies ran while one was open for 44% of the time, Pallas kernels for 0%

commit v1 on v0

--- a/solution.py
+++ b/solution.py
@@ -1,6 +1,10 @@
+import functools
+
 import jax
 import jax.numpy as jnp
 from jax import lax
+from jax.experimental import pallas as pl
+from jax.experimental.pallas import tpu as pltpu
 from jax.sharding import PartitionSpec as P
 
 
@@ -63,7 +67,7 @@
     return tuple((right_one for right_one in right_parts))
 
 
-def per_device(
+def per_device_general(
     cotangent,
     wigner,
     sender_ids,
@@ -151,6 +155,347 @@
     return result.reshape(coef_rows, chan_share, atom_share)
 
 
+MESH = pl.DeviceIdType.MESH
+F32 = jnp.float32
+BF16 = jnp.bfloat16
+
+
+def dot_last(left, right):
+    return lax.dot_general(left, right, (((1,), (1,)), ((), ())), preferred_element_type=F32)
+
+
+def dot_first(left, right):
+    return lax.dot_general(left, right, (((0,), (0,)), ((), ())), preferred_element_type=F32)
+
+
+def rotate_chunk(grads, wig, rotated, columns):
+    offset = 0
+    for degree in range(7):
+        reach = min(degree, 2)
+        starts = {-2: 22 + degree, -1: 12 + degree, 0: degree, 1: 6 + degree, 2: 17 + degree}
+        rows = [grads[pl.ds(64 * starts[m], 64), columns] for m in range(-reach, reach + 1)]
+        width = 2 * degree + 1
+        for p in range(width):
+            total = None
+            for position, row in enumerate(rows):
+                at = offset + position * width + p
+                term = wig[at : at + 1, columns] * row
+                total = term if total is None else total + term
+            total = total.astype(BF16)
+            for half in range(4):
+                rotated[
+                    half // 2, half % 2, degree * degree + p, :, columns
+                ] = total[16 * half : 16 * half + 16]
+        offset += len(rows) * width
+
+
+def fused_kernel(
+    chunks,
+    cot,
+    wigner,
+    senders,
+    slots,
+    dests,
+    lives,
+    lists,
+    wzero,
+    wone,
+    wtwo,
+    to_grid,
+    from_grid,
+    pre,
+    out,
+    gathered,
+    grads,
+    wig,
+    rotated,
+    hot_recv,
+    hot_send,
+    acc_recv,
+    acc_send,
+    send_to,
+    recv_to,
+    message,
+    arrived,
+    slope,
+    packed,
+    tall,
+    flat,
+    local_sem,
+    out_sem,
+    in_sem,
+    far_out,
+    far_in,
+):
+    x = lax.axis_index("chan")
+    core = lax.axis_index("sub")
+    z = lax.axis_index("atoms")
+    shards = message.shape[0]
+    atoms = acc_send.shape[1]
+    me, xpart = 2 * x + core, 2 * (1 - x) + core
+    cpart, dpart = 2 * x + 1 - core, 2 * (1 - x) + 1 - core
+    to_core, to_chip = {"sub": 1 - core}, {"chan": 1 - x}
+    edges = cot.shape[2]
+    wide = edges // chunks
+
+    barrier = pltpu.get_barrier_semaphore()
+    pl.semaphore_signal(barrier, inc=1, device_id=to_core, device_id_type=MESH)
+    pl.semaphore_signal(barrier, inc=1, device_id=to_chip, device_id_type=MESH)
+    for step in range(1, shards):
+        pl.semaphore_signal(
+            barrier, inc=1, device_id={"atoms": lax.rem(z + step, shards)}, device_id_type=MESH
+        )
+    pl.semaphore_wait(barrier, shards + 1)
+
+    def span(j):
+        return pl.ds(pl.multiple_of(j * wide, wide), wide)
+
+    def own_copy(j, kind, target):
+        return pltpu.make_async_remote_copy(
+            src_ref=cot.at[:, :, span(j)],
+            dst_ref=gathered.at[:, me, :, span(j)],
+            send_sem=out_sem.at[kind, j],
+            recv_sem=in_sem.at[kind, j],
+            device_id=target,
+            device_id_type=MESH,
+        )
+
+    def arrival(j, kind, origin, target):
+        return pltpu.make_async_remote_copy(
+            src_ref=gathered.at[:, origin, :, span(j)],
+            dst_ref=gathered.at[:, origin, :, span(j)],
+            send_sem=out_sem.at[kind, j],
+            recv_sem=in_sem.at[kind, j],
+            device_id=target,
+            device_id_type=MESH,
+        )
+
+    def start_chunk(j, carry):
+        own_copy(j, 1, to_chip).start()
+        own_copy(j, 0, to_core).start()
+        return carry
+
+    lax.fori_loop(0, chunks, start_chunk, 0)
+    keep = pltpu.make_async_copy(cot, gathered.at[:, me], local_sem)
+    keep.start()
+
+    blocks, block = slots.shape
+    live = lax.broadcasted_iota(jnp.int32, (blocks, block), 1) < lives[...]
+    listed = jnp.zeros((blocks, block), jnp.int32)
+    for slot in range(lists.shape[1]):
+        listed = jnp.where(slots[...] == slot, lists[:, slot : slot + 1], listed)
+    recv_to[...] = jnp.where(live, dests[...] * atoms + listed, -1)
+    send_to[...] = jnp.where(live, senders[...], -1)
+    acc_recv[...] = jnp.zeros_like(acc_recv)
+    acc_send[...] = jnp.zeros_like(acc_send)
+
+    packed[:, 0:atoms] = pre[...].astype(F32)
+    packed[:, atoms:128] = jnp.zeros((packed.shape[0], 128 - atoms), F32)
+    coefs = to_grid.shape[1]
+    for c in range(16):
+        pair = [
+            packed[pl.ds(16 * half + c, coefs, stride=32), :][:, 0:atoms] for half in range(2)
+        ]
+        flat[:, 128 * c : 128 * c + 128] = jnp.concatenate(pair, axis=1).astype(BF16)
+
+    def slope_part(i, carry):
+        columns = pl.ds(pl.multiple_of(i * 256, 256), 256)
+        value = jnp.dot(to_grid[...], flat[:, columns], preferred_element_type=F32)
+        sig = 1.0 / (1.0 + jnp.exp(-value))
+        slope[:, columns] = sig * (1.0 + value * (1.0 - sig))
+        return carry
+
+    lax.fori_loop(0, 8, slope_part, 0)
+    keep.wait()
+
+    def work(j, carry):
+        arrival(j, 1, xpart, to_chip).wait_recv()
+        arrival(j, 2, xpart, to_core).start()
+        arrival(j, 0, cpart, to_core).wait_recv()
+        arrival(j, 2, dpart, to_core).wait_recv()
+        piece = gathered[:, :, :, span(j)].reshape(29 * 64, wide)
+        grads[0:448] = jnp.dot(wzero[...], piece[0:448], preferred_element_type=F32)
+        grads[448:1216] = jnp.dot(wone[...], piece[448:1216], preferred_element_type=F32)
+        grads[1216:1856] = jnp.dot(wtwo[...], piece[1216:1856], preferred_element_type=F32)
+        wig[...] = wigner[:, span(j)].astype(F32)
+
+        for i in range(wide // block):
+            columns = pl.ds(i * block, block)
+            rotate_chunk(grads, wig, rotated, columns)
+            row = pl.ds(j * (wide // block) + i, 1)
+            hot_recv[:, columns] = (
+                lax.broadcasted_iota(jnp.int32, (hot_recv.shape[0], block), 0) == recv_to[row, :]
+            ).astype(F32).astype(BF16)
+            hot_send[:, columns] = (
+                lax.broadcasted_iota(jnp.int32, (hot_send.shape[0], block), 0) == send_to[row, :]
+            ).astype(F32).astype(BF16)
+        height = acc_recv.shape[0]
+        acc_recv[...] += dot_last(rotated[1].reshape(height, wide), hot_recv[...])
+        acc_send[...] += dot_last(rotated[0].reshape(height, wide), hot_send[...])
+        return carry
+
+    lax.fori_loop(0, chunks, work, 0)
+
+    half_rows = acc_recv.shape[0] // 2
+    for d in range(shards):
+        cut = slice(atoms * d, atoms * d + atoms)
+        message[d] = jnp.concatenate(
+            [acc_recv[0:half_rows, cut], acc_recv[half_rows:, cut]], axis=1
+        ).astype(BF16)
+
+    def far_copy(step):
+        return pltpu.make_async_remote_copy(
+            src_ref=message.at[lax.rem(z + step, shards)],
+            dst_ref=arrived.at[step - 1],
+            send_sem=far_out.at[step - 1],
+            recv_sem=far_in.at[step - 1],
+            device_id={"atoms": lax.rem(z + step, shards)},
+            device_id_type=MESH,
+        )
+
+    for step in range(1, shards):
+        far_copy(step).start()
+    total = jnp.concatenate([acc_send[0:half_rows], acc_send[half_rows:]], axis=1)
+    total = total + message[z].astype(F32)
+    for step in range(1, shards):
+        far_copy(step).wait_recv()
+        total = total + arrived[step - 1].astype(F32)
+    tall[...] = total
+    for c in range(16):
+        flat[:, 128 * c : 128 * c + 128] = tall[pl.ds(c, coefs, stride=16), :].astype(BF16)
+    for i in range(8):
+        columns = slice(256 * i, 256 * i + 256)
+        term = (slope[:, columns] * dot_first(from_grid[...], flat[:, columns])).astype(BF16)
+        result = dot_first(to_grid[...], term)
+        for c in range(2):
+            tall[pl.ds(2 * i + c, coefs, stride=16), :] = result[:, 128 * c : 128 * c + 128]
+    done = tall[...].astype(BF16).reshape(coefs, 16, 128)
+    out[:, 0:16, :] = done[:, :, 0:atoms]
+    out[:, 16:32, :] = done[:, :, atoms:128]
+
+    def finish(j, carry):
+        own_copy(j, 1, to_chip).wait_send()
+        own_copy(j, 0, to_core).wait_send()
+        arrival(j, 2, xpart, to_core).wait_send()
+        return carry
+
+    lax.fori_loop(0, chunks, finish, 0)
+    for step in range(1, shards):
+        far_copy(step).wait_send()
+
+
+def per_device(
+    mesh,
+    cotangent,
+    wigner,
+    sender_ids,
+    receiver_slots,
+    destinations,
+    live_counts,
+    receiver_lists,
+    weight_zero,
+    real_one,
+    imag_one,
+    real_two,
+    imag_two,
+    to_grid,
+    from_grid,
+    pre_act,
+):
+    edges = cotangent.shape[2]
+    blocks = destinations.shape[0]
+    block = edges // blocks
+    coefs, chan_share, atoms = pre_act.shape
+    shards = mesh.shape["atoms"]
+    fits = (
+        mesh.shape["chan"] == 2
+        and mesh.shape["sub"] == 2
+        and cotangent.shape[1] == 16
+        and chan_share == 32
+        and atoms == 64
+        and block == 128
+        and blocks % 2 == 0
+        and 1 < shards <= 4
+    )
+    if not fits:
+        return per_device_general(
+            cotangent,
+            wigner,
+            sender_ids,
+            receiver_slots,
+            destinations,
+            live_counts,
+            receiver_lists,
+            weight_zero,
+            real_one,
+            imag_one,
+            real_two,
+            imag_two,
+            to_grid,
+            from_grid,
+            pre_act,
+        )
+
+    def paired(real, imag):
+        size = real.shape[0] * 64
+        real, imag = real.reshape(size, size), imag.reshape(size, size)
+        return jnp.concatenate(
+            [jnp.concatenate([real, imag], axis=1), jnp.concatenate([-imag, real], axis=1)], axis=0
+        )
+
+    chunks = blocks // 2
+    wide = 2 * block
+    height = coefs * chan_share
+    points = to_grid.shape[0]
+    vmem = pl.BlockSpec(memory_space=pltpu.VMEM)
+    return pl.pallas_call(
+        functools.partial(fused_kernel, chunks),
+        out_shape=jax.ShapeDtypeStruct(pre_act.shape, BF16),
+        in_specs=[vmem] * 13,
+        out_specs=vmem,
+        scratch_shapes=[
+            pltpu.VMEM((29, 4, 16, edges), BF16),
+            pltpu.VMEM((29 * 64, wide), F32),
+            pltpu.VMEM((wigner.shape[0], wide), F32),
+            pltpu.VMEM((2, 2, coefs, 16, wide), BF16),
+            pltpu.VMEM((shards * atoms, wide), BF16),
+            pltpu.VMEM((atoms, wide), BF16),
+            pltpu.VMEM((height, shards * atoms), F32),
+            pltpu.VMEM((height, atoms), F32),
+            pltpu.VMEM((blocks, block), jnp.int32),
+            pltpu.VMEM((blocks, block), jnp.int32),
+            pltpu.VMEM((shards, height // 2, 2 * atoms), BF16),
+            pltpu.VMEM((shards - 1, height // 2, 2 * atoms), BF16),
+            pltpu.VMEM((points, chan_share * atoms), F32),
+            pltpu.VMEM((height, 128), F32),
+            pltpu.VMEM((height // 2, 128), F32),
+            pltpu.VMEM((coefs, chan_share * atoms), BF16),
+            pltpu.SemaphoreType.DMA,
+            pltpu.SemaphoreType.DMA((3, chunks)),
+            pltpu.SemaphoreType.DMA((3, chunks)),
+            pltpu.SemaphoreType.DMA((shards - 1,)),
+            pltpu.SemaphoreType.DMA((shards - 1,)),
+        ],
+        compiler_params=pltpu.CompilerParams(
+            collective_id=0, has_side_effects=True, vmem_limit_bytes=50 * 2**20
+        ),
+    )(
+        cotangent,
+        wigner,
+        sender_ids.reshape(blocks, block),
+        receiver_slots.reshape(blocks, block),
+        destinations.reshape(blocks, 1),
+        live_counts.reshape(blocks, 1),
+        receiver_lists,
+        weight_zero.reshape(448, 448),
+        paired(real_one, imag_one),
+        paired(real_two, imag_two),
+        to_grid,
+        from_grid,
+        pre_act.reshape(height, atoms),
+    )
+
+
 def solution(mesh):
     in_specs = (
         P(None, ("chan", "sub"), ("groups", "atoms")),
@@ -171,5 +516,5 @@
     )
     out_specs = P(None, ("chan", "sub"), ("groups", "atoms"))
     return jax.shard_map(
-        per_device, mesh=mesh, in_specs=in_specs, out_specs=out_specs, check_vma=False
-    )
+        functools.partial(per_device, mesh), mesh=mesh, in_specs=in_specs, out_specs=out_specs, check_vma=False
+    )

time: 155 us -> 73.6 us (0.47)
  the two profiles are of different devices: /device:TPU:0 before, /device:TPU:9 now
where the time goes in v1:
time: 73.6 us; the launch traced here: 73.3 us
  Pallas kernels  61.6 us (84%)
  local copies, waits for them, and re-layouts  9.92 us (13%)
  other arithmetic  1.52 us (2%)
    pallas_call x1, Pallas kernels, per_device(): pl.pallas_call(functools.partial(fused_kernel, chunks), out_shape=jax.Sha...  61.6 us
    unnamed x29, local copies, waits for them, and re-layouts  5.59 us
    reshape x4, local copies, waits for them, and re-layouts, paired(): real, imag = (real.reshape(size, size), imag.reshape(size, size))  2.41 us

profile of v1, /device:TPU:9, one launch (start us, length us, event | category | flops | bytes accessed | tf_op | source)
XLA Modules:
  0.0 73.3 jit_solution(10502773186986764793)
XLA Ops:
  0.0 0.7 %copy.29.dests = s32[12,1]{1,0:T(8,128)S(1)} copy(s32[12,1]{0,1:T(1,128)} %bitcast.8) | data formatting | bytes 96 | tf_op jit(solution)/shard_map/reshape | solution.py:487
  0.7 0.7 %copy.30.lives = s32[12,1]{1,0:T(8,128)S(1)} copy(s32[12,1]{0,1:T(1,128)} %bitcast.9) | data formatting | bytes 96 | tf_op jit(solution)/shard_map/reshape | solution.py:488
  1.5 0.0 copy-start.6
  1.5 1.6 %copy.24 = bf16[7,2,32,7,64]{4,3,2,1,0:T(8,128)(2,1)S(1)} copy(bf16[7,2,32,7,64]{4,2,3,1,0:T(8,128)(2,1)} %param.22) | data formatting | bytes 802816 | tf_op args[7]
  3.1 0.4 reshape.34.wzero
  3.5 0.0 copy-done.6
  3.5 0.0 copy-start.7
  3.5 0.3 copy.25
  3.8 0.5 reshape.35
  4.3 0.3 copy-done.7
  4.6 0.3 copy.26
  4.9 0.5 reshape.36
  5.3 0.0 copy-start.8
  5.4 0.1 neg.6
  5.4 0.1 maximum_maximum_fusion.wone
  5.5 0.8 %copy-done.8 = bf16[5,2,32,5,64]{4,2,3,1,0:T(8,128)(2,1)S(1)} copy-done((bf16[5,2,32,5,64]{4,2,3,1,0:T(8,128)(2,1)S(1)}, bf16[5,2,32,5,64]{4,2,3,1,0:T(8,128)(2,1)}, u32[]{:S(2)}) %copy-start.8) | copy-done | bytes 204824
  6.3 0.0 copy-start.9
  6.3 0.2 copy.27
  6.6 1.1 %reshape.37 = bf16[320,320]{1,0:T(8,128)(2,1)} reshape(bf16[5,2,32,5,64]{4,3,2,1,0:T(8,128)(2,1)S(1)} %copy.27) | data formatting | bytes 409600 | tf_op jit(solution)/shard_map/reshape | solution.py:441
  7.6 0.0 copy-done.9
  7.7 0.2 copy.28
  7.9 0.0 copy-start.10
  7.9 0.0 copy-start
  7.9 0.0 copy-start.2
  7.9 0.0 copy-start.3
  7.9 0.0 copy-start.4
  7.9 0.0 copy-start.5
  7.9 0.4 reshape.38
  8.4 1.3 %maximum_maximum_fusion.1.wtwo = bf16[640,640]{1,0:T(8,128)(2,1)S(1)} fusion(bf16[320,320]{1,0:T(8,128)(2,1)} %reshape.37, bf16[320,320]{1,0:T(8,128)(2,1)S(1)} %neg.7, bf16[320,320]{1,0:T(8,128)(2,1)S(1)} %reshape.38), kind=kLoop, calls=%fused_computation.1 | loop fusion | flops 3276800 | bytes 1433600 | tf_op jit(solution)/shard_map/concatenate | solution.py:442
  9.7 0.0 copy-done.10
  9.7 0.1 copy.31.to_grid
  9.8 0.0 copy-done
  9.8 0.0 copy-done.2
  9.8 0.0 copy-done.3
  9.9 0.0 copy-done.4
  9.9 0.0 copy-done.5
  9.9 0.0 copy-start.1
  9.9 1.0 %copy-done.1 = bf16[49,32,64]{2,1,0:T(8,128)(2,1)S(1)} copy-done((bf16[49,32,64]{2,1,0:T(8,128)(2,1)S(1)}, bf16[49,32,64]{2,1,0:T(8,128)(2,1)}, u32[]{:S(2)}) %copy-start.1) | copy-done | bytes 200728
  10.9 61.6 %shard_map.145 = bf16[49,32,64]{2,1,0:T(8,128)(2,1)S(1)} custom-call(bf16[29,16,1536]{2,1,0:T(8,128)(2,1)} %cot.1, bf16[235,1536]{1,0:T(8,128)(2,1)S(1)} %copy-done, s32[12,128]{1,0:T(8,128)S(1)} %bitcast.6, s32[12,128]{1,0:T(8,128)S(1)} %bitcast.7, s32[12,1]{1,0:T(8,128)S(1)} %copy.29.dests, s32[12,1]{1,0:T(8,128)S(1)} %copy.30.lives, ...), custom_call_target="tpu_custom_call" | custom-call | tf_op jit(solution)/shard_map/pallas_call | solution.py:451
  72.5 0.8 %copy.33 = bf16[49,32,64]{2,1,0:T(8,128)(2,1)} copy(bf16[49,32,64]{2,1,0:T(8,128)(2,1)S(1)} %shard_map.145) | data formatting | bytes 401408
  (1 shorter events, 0.0 us)
Async XLA Ops:
  1.5 2.0 %copy-start.6 = (bf16[6,2,32,6,64]{4,2,3,1,0:T(8,128)(2,1)S(1)}, bf16[6,2,32,6,64]{4,2,3,1,0:T(8,128)(2,1)}, u32[]{:S(2)}) copy-start(bf16[6,2,32,6,64]{4,2,3,1,0:T(8,128)(2,1)} %param.23) | copy-start | bytes 884740
  3.5 1.1 %copy-start.7 = (bf16[6,2,32,6,64]{4,2,3,1,0:T(8,128)(2,1)S(1)}, bf16[6,2,32,6,64]{4,2,3,1,0:T(8,128)(2,1)}, u32[]{:S(2)}) copy-start(bf16[6,2,32,6,64]{4,2,3,1,0:T(8,128)(2,1)} %param.24) | copy-start | bytes 884740
  5.3 1.0 %copy-start.8 = (bf16[5,2,32,5,64]{4,2,3,1,0:T(8,128)(2,1)S(1)}, bf16[5,2,32,5,64]{4,2,3,1,0:T(8,128)(2,1)}, u32[]{:S(2)}) copy-start(bf16[5,2,32,5,64]{4,2,3,1,0:T(8,128)(2,1)} %param.25) | copy-start | bytes 614404
  6.3 1.3 %copy-start.9 = (bf16[5,2,32,5,64]{4,2,3,1,0:T(8,128)(2,1)S(1)}, bf16[5,2,32,5,64]{4,2,3,1,0:T(8,128)(2,1)}, u32[]{:S(2)}) copy-start(bf16[5,2,32,5,64]{4,2,3,1,0:T(8,128)(2,1)} %param.26) | copy-start | bytes 614404
  7.9 1.8 %copy-start.10 = (bf16[196,49]{0,1:T(8,128)(2,1)S(1)}, bf16[196,49]{0,1:T(8,128)(2,1)}, u32[]{:S(2)}) copy-start(bf16[196,49]{0,1:T(8,128)(2,1)} %param.27) | copy-start | bytes 57628
  7.9 2.0 %copy-start = (bf16[235,1536]{1,0:T(8,128)(2,1)S(1)}, bf16[235,1536]{1,0:T(8,128)(2,1)}, u32[]{:S(2)}) copy-start(bf16[235,1536]{1,0:T(8,128)(2,1)} %wigner.1) | copy-start | bytes 2165764
  7.9 1.9 %copy-start.2 = (bf16[49,196]{1,0:T(8,128)(2,1)S(1)}, bf16[49,196]{1,0:T(8,128)(2,1)}, u32[]{:S(2)}) copy-start(bf16[49,196]{1,0:T(8,128)(2,1)} %from_grid.1) | copy-start | bytes 57628
  7.9 1.9 %copy-start.3 = (s32[1536]{0:T(1024)S(1)}, s32[1536]{0:T(1024)}, u32[]{:S(2)}) copy-start(s32[1536]{0:T(1024)} %param.17) | copy-start | bytes 18436
  7.9 1.9 %copy-start.4 = (s32[1536]{0:T(1024)S(1)}, s32[1536]{0:T(1024)}, u32[]{:S(2)}) copy-start(s32[1536]{0:T(1024)} %param.18) | copy-start | bytes 18436
  7.9 1.9 %copy-start.5 = (s32[12,32]{1,0:T(8,128)S(1)}, s32[12,32]{1,0:T(8,128)}, u32[]{:S(2)}) copy-start(s32[12,32]{1,0:T(8,128)} %lists.1) | copy-start | bytes 4612
  9.9 1.0 %copy-start.1 = (bf16[49,32,64]{2,1,0:T(8,128)(2,1)S(1)}, bf16[49,32,64]{2,1,0:T(8,128)(2,1)}, u32[]{:S(2)}) copy-start(bf16[49,32,64]{2,1,0:T(8,128)(2,1)} %param.29) | copy-start | bytes 602116

commit v2 on v1

--- a/solution.py
+++ b/solution.py
@@ -189,23 +189,47 @@
         offset += len(rows) * width
 
 
+def spread(raw, total, top, left, sign):
+    outs, halves, ins, rows, width = raw.shape
+
+    def one(i, carry):
+        a, h = lax.div(i, halves), lax.rem(i, halves)
+        at = pl.ds(pl.multiple_of(top + i * rows, rows), rows)
+        for b in range(ins):
+            piece = raw[a, h, b]
+            total[at, left + b * width : left + b * width + width] = piece if sign > 0 else -piece
+        return carry
+
+    lax.fori_loop(0, outs * halves, one, 0)
+
+
 def fused_kernel(
     chunks,
     cot,
-    wigner,
+    wigner_hbm,
     senders,
     slots,
     dests,
     lives,
     lists,
+    weight_zero,
+    real_one,
+    imag_one,
+    real_two,
+    imag_two,
+    grid_to,
+    from_grid,
+    pre_hbm,
+    out,
+    gathered,
+    wigner,
+    raw_zero,
+    raw_one,
+    raw_two,
     wzero,
     wone,
     wtwo,
-    to_grid,
-    from_grid,
     pre,
-    out,
-    gathered,
     grads,
     wig,
     rotated,
@@ -276,22 +300,39 @@
         return carry
 
     lax.fori_loop(0, chunks, start_chunk, 0)
-    keep = pltpu.make_async_copy(cot, gathered.at[:, me], local_sem)
-    keep.start()
+    loads = [
+        (pre_hbm, pre),
+        (weight_zero, raw_zero),
+        (real_one, raw_one.at[0]),
+        (imag_one, raw_one.at[1]),
+        (real_two, raw_two.at[0]),
+        (imag_two, raw_two.at[1]),
+        (wigner_hbm, wigner),
+        (cot, gathered.at[:, me]),
+    ]
+    loads = [
+        pltpu.make_async_copy(origin, target, local_sem.at[i])
+        for i, (origin, target) in enumerate(loads)
+    ]
+    for load in loads:
+        load.start()
 
     blocks, block = slots.shape
-    live = lax.broadcasted_iota(jnp.int32, (blocks, block), 1) < lives[...]
     listed = jnp.zeros((blocks, block), jnp.int32)
     for slot in range(lists.shape[1]):
         listed = jnp.where(slots[...] == slot, lists[:, slot : slot + 1], listed)
-    recv_to[...] = jnp.where(live, dests[...] * atoms + listed, -1)
-    send_to[...] = jnp.where(live, senders[...], -1)
+    for b in range(blocks):
+        live = lax.broadcasted_iota(jnp.int32, (1, block), 1) < lives[b]
+        at = slice(b, b + 1)
+        recv_to[at, :] = jnp.where(live, dests[b] * atoms + listed[at], -1)
+        send_to[at, :] = jnp.where(live, senders[at, :], -1)
     acc_recv[...] = jnp.zeros_like(acc_recv)
     acc_send[...] = jnp.zeros_like(acc_send)
 
+    loads[0].wait()
     packed[:, 0:atoms] = pre[...].astype(F32)
     packed[:, atoms:128] = jnp.zeros((packed.shape[0], 128 - atoms), F32)
-    coefs = to_grid.shape[1]
+    coefs = grid_to.shape[0]
     for c in range(16):
         pair = [
             packed[pl.ds(16 * half + c, coefs, stride=32), :][:, 0:atoms] for half in range(2)
@@ -300,13 +341,21 @@
 
     def slope_part(i, carry):
         columns = pl.ds(pl.multiple_of(i * 256, 256), 256)
-        value = jnp.dot(to_grid[...], flat[:, columns], preferred_element_type=F32)
+        value = dot_first(grid_to[...], flat[:, columns])
         sig = 1.0 / (1.0 + jnp.exp(-value))
         slope[:, columns] = sig * (1.0 + value * (1.0 - sig))
         return carry
 
     lax.fori_loop(0, 8, slope_part, 0)
-    keep.wait()
+    for load in loads[1:]:
+        load.wait()
+    spread(raw_zero, wzero, 0, 0, 1)
+    for both, total in ((raw_one, wone), (raw_two, wtwo)):
+        size = total.shape[0] // 2
+        spread(both.at[0], total, 0, 0, 1)
+        spread(both.at[1], total, 0, size, 1)
+        spread(both.at[1], total, size, 0, -1)
+        spread(both.at[0], total, size, size, 1)
 
     def work(j, carry):
         arrival(j, 1, xpart, to_chip).wait_recv()
@@ -366,7 +415,7 @@
     for i in range(8):
         columns = slice(256 * i, 256 * i + 256)
         term = (slope[:, columns] * dot_first(from_grid[...], flat[:, columns])).astype(BF16)
-        result = dot_first(to_grid[...], term)
+        result = jnp.dot(grid_to[...], term, preferred_element_type=F32)
         for c in range(2):
             tall[pl.ds(2 * i + c, coefs, stride=16), :] = result[:, 128 * c : 128 * c + 128]
     done = tall[...].astype(BF16).reshape(coefs, 16, 128)
@@ -436,25 +485,32 @@
             pre_act,
         )
 
-    def paired(real, imag):
-        size = real.shape[0] * 64
-        real, imag = real.reshape(size, size), imag.reshape(size, size)
-        return jnp.concatenate(
-            [jnp.concatenate([real, imag], axis=1), jnp.concatenate([-imag, real], axis=1)], axis=0
-        )
-
+    weights = [
+        weight.transpose(0, 1, 3, 2, 4)
+        for weight in (weight_zero, real_one, imag_one, real_two, imag_two)
+    ]
     chunks = blocks // 2
     wide = 2 * block
     height = coefs * chan_share
     points = to_grid.shape[0]
     vmem = pl.BlockSpec(memory_space=pltpu.VMEM)
+    smem = pl.BlockSpec(memory_space=pltpu.SMEM)
+    hbm = pl.BlockSpec(memory_space=pltpu.HBM)
     return pl.pallas_call(
         functools.partial(fused_kernel, chunks),
         out_shape=jax.ShapeDtypeStruct(pre_act.shape, BF16),
-        in_specs=[vmem] * 13,
+        in_specs=[hbm, hbm, vmem, vmem, smem, smem, vmem] + [hbm] * 5 + [vmem, vmem, hbm],
         out_specs=vmem,
         scratch_shapes=[
             pltpu.VMEM((29, 4, 16, edges), BF16),
+            pltpu.VMEM(wigner.shape, BF16),
+            pltpu.VMEM(weights[0].shape, BF16),
+            pltpu.VMEM((2,) + weights[1].shape, BF16),
+            pltpu.VMEM((2,) + weights[3].shape, BF16),
+            pltpu.VMEM((448, 448), BF16),
+            pltpu.VMEM((768, 768), BF16),
+            pltpu.VMEM((640, 640), BF16),
+            pltpu.VMEM((height, atoms), BF16),
             pltpu.VMEM((29 * 64, wide), F32),
             pltpu.VMEM((wigner.shape[0], wide), F32),
             pltpu.VMEM((2, 2, coefs, 16, wide), BF16),
@@ -470,27 +526,25 @@
             pltpu.VMEM((height, 128), F32),
             pltpu.VMEM((height // 2, 128), F32),
             pltpu.VMEM((coefs, chan_share * atoms), BF16),
-            pltpu.SemaphoreType.DMA,
+            pltpu.SemaphoreType.DMA((8,)),
             pltpu.SemaphoreType.DMA((3, chunks)),
             pltpu.SemaphoreType.DMA((3, chunks)),
             pltpu.SemaphoreType.DMA((shards - 1,)),
             pltpu.SemaphoreType.DMA((shards - 1,)),
         ],
         compiler_params=pltpu.CompilerParams(
-            collective_id=0, has_side_effects=True, vmem_limit_bytes=50 * 2**20
+            collective_id=0, has_side_effects=True, vmem_limit_bytes=62 * 2**20
         ),
     )(
         cotangent,
         wigner,
         sender_ids.reshape(blocks, block),
         receiver_slots.reshape(blocks, block),
-        destinations.reshape(blocks, 1),
-        live_counts.reshape(blocks, 1),
+        destinations,
+        live_counts,
         receiver_lists,
-        weight_zero.reshape(448, 448),
-        paired(real_one, imag_one),
-        paired(real_two, imag_two),
-        to_grid,
+        *weights,
+        to_grid.T,
         from_grid,
         pre_act.reshape(height, atoms),
     )

time: 73.6 us -> 64.2 us (0.87)
  local copies, waits for them, and re-layouts: 9.92 us -> 1.77 us
  other arithmetic: 1.52 us -> 0 us
    reshape x7 -> x0, local copies, waits for them, and re-layouts: 4.34 us -> none  [the longest x4 2.41 us: paired(): real, imag = (real.reshape(size, size), imag.reshape(size, size))]
    unnamed x29 -> x1, local copies, waits for them, and re-layouts: 5.59 us -> 1.77 us
    concatenate x2 -> x0, other arithmetic: 1.42 us -> none  [paired(): jnp.concatenate([jnp.concatenate([real, imag], axis=1), jnp.concatenate([...]
where the time goes in v2:
time: 64.2 us; the launch traced here: 63.9 us
  Pallas kernels  62.2 us (97%)
  local copies, waits for them, and re-layouts  1.77 us (3%)
    pallas_call x1, Pallas kernels, per_device(): pl.pallas_call(functools.partial(fused_kernel, chunks), out_shape=jax.Sha...  62.2 us
    unnamed x1, local copies, waits for them, and re-layouts  1.77 us

profile of v2, /device:TPU:9, one launch (start us, length us, event | category | flops | bytes accessed | tf_op | source)
XLA Modules:
  0.0 63.9 jit_solution(11318372704818527718)
XLA Ops:
  0.0 62.2 %shard_map.145 = bf16[49,32,64]{2,1,0:T(8,128)(2,1)} custom-call(bf16[29,16,1536]{2,1,0:T(8,128)(2,1)} %cot.1, bf16[235,1536]{1,0:T(8,128)(2,1)} %wigner_hbm.1, s32[12,128]{1,0:T(8,128)} %bitcast.16, s32[12,128]{1,0:T(8,128)} %bitcast.17, s32[12]{0:T(128)} %dests.1, s32[12]{0:T(128)} %lives.1, s32[12,32]{1,0:T(8,128)} %lists.1, ...), custom_call_target="tpu_custom_call" | custom-call | tf_op jit(solution)/shard_map/pallas_call | solution.py:499
  62.2 1.8 %copy.17 = bf16[49,32,64]{2,1,0:T(8,128)(2,1)} copy(bf16[49,32,64]{2,1,0:T(8,128)(2,1)} %shard_map.145) | data formatting | bytes 401408

commit v3 on v2

--- a/solution.py
+++ b/solution.py
@@ -158,6 +158,8 @@
 MESH = pl.DeviceIdType.MESH
 F32 = jnp.float32
 BF16 = jnp.bfloat16
+PARTS = (range(0, 4), range(4, 5), range(5, 6), range(6, 7))
+STEPS = {2: (1,), 3: (1, 2), 4: (2, 1, 3)}
 
 
 def dot_last(left, right):
@@ -168,10 +170,10 @@
     return lax.dot_general(left, right, (((0,), (0,)), ((), ())), preferred_element_type=F32)
 
 
-def rotate_chunk(grads, wig, rotated, columns):
-    offset = 0
-    for degree in range(7):
+def rotate_chunk(grads, wig, rotated, columns, degrees=range(7)):
+    for degree in degrees:
         reach = min(degree, 2)
+        offset = sum((2 * min(k, 2) + 1) * (2 * k + 1) for k in range(degree))
         starts = {-2: 22 + degree, -1: 12 + degree, 0: degree, 1: 6 + degree, 2: 17 + degree}
         rows = [grads[pl.ds(64 * starts[m], 64), columns] for m in range(-reach, reach + 1)]
         width = 2 * degree + 1
@@ -186,7 +188,6 @@
                 rotated[
                     half // 2, half % 2, degree * degree + p, :, columns
                 ] = total[16 * half : 16 * half + 16]
-        offset += len(rows) * width
 
 
 def spread(raw, total, top, left, sign):
@@ -357,20 +358,26 @@
         spread(both.at[1], total, size, 0, -1)
         spread(both.at[0], total, size, size, 1)
 
-    def work(j, carry):
+    half_rows = acc_recv.shape[0] // 2
+
+    def far_copy(step, part):
+        first, last = PARTS[part][0] ** 2, PARTS[part][-1] ** 2 + 2 * PARTS[part][-1] + 1
+        rows = pl.ds(16 * first, 16 * (last - first))
+        return pltpu.make_async_remote_copy(
+            src_ref=message.at[lax.rem(z + step, shards), rows],
+            dst_ref=arrived.at[step - 1, rows],
+            send_sem=far_out.at[step - 1, part],
+            recv_sem=far_in.at[step - 1, part],
+            device_id={"atoms": lax.rem(z + step, shards)},
+            device_id_type=MESH,
+        )
+
+    def prepare(j):
         arrival(j, 1, xpart, to_chip).wait_recv()
         arrival(j, 2, xpart, to_core).start()
-        arrival(j, 0, cpart, to_core).wait_recv()
-        arrival(j, 2, dpart, to_core).wait_recv()
-        piece = gathered[:, :, :, span(j)].reshape(29 * 64, wide)
-        grads[0:448] = jnp.dot(wzero[...], piece[0:448], preferred_element_type=F32)
-        grads[448:1216] = jnp.dot(wone[...], piece[448:1216], preferred_element_type=F32)
-        grads[1216:1856] = jnp.dot(wtwo[...], piece[1216:1856], preferred_element_type=F32)
         wig[...] = wigner[:, span(j)].astype(F32)
-
         for i in range(wide // block):
             columns = pl.ds(i * block, block)
-            rotate_chunk(grads, wig, rotated, columns)
             row = pl.ds(j * (wide // block) + i, 1)
             hot_recv[:, columns] = (
                 lax.broadcasted_iota(jnp.int32, (hot_recv.shape[0], block), 0) == recv_to[row, :]
@@ -378,38 +385,52 @@
             hot_send[:, columns] = (
                 lax.broadcasted_iota(jnp.int32, (hot_send.shape[0], block), 0) == send_to[row, :]
             ).astype(F32).astype(BF16)
+        arrival(j, 0, cpart, to_core).wait_recv()
+        arrival(j, 2, dpart, to_core).wait_recv()
+        piece = gathered[:, :, :, span(j)].reshape(29 * 64, wide)
+        grads[0:448] = jnp.dot(wzero[...], piece[0:448], preferred_element_type=F32)
+        grads[448:1216] = jnp.dot(wone[...], piece[448:1216], preferred_element_type=F32)
+        grads[1216:1856] = jnp.dot(wtwo[...], piece[1216:1856], preferred_element_type=F32)
+
+    def work(j, carry):
+        prepare(j)
+        for i in range(wide // block):
+            rotate_chunk(grads, wig, rotated, pl.ds(i * block, block))
         height = acc_recv.shape[0]
         acc_recv[...] += dot_last(rotated[1].reshape(height, wide), hot_recv[...])
         acc_send[...] += dot_last(rotated[0].reshape(height, wide), hot_send[...])
         return carry
 
-    lax.fori_loop(0, chunks, work, 0)
-
-    half_rows = acc_recv.shape[0] // 2
-    for d in range(shards):
-        cut = slice(atoms * d, atoms * d + atoms)
-        message[d] = jnp.concatenate(
-            [acc_recv[0:half_rows, cut], acc_recv[half_rows:, cut]], axis=1
-        ).astype(BF16)
-
-    def far_copy(step):
-        return pltpu.make_async_remote_copy(
-            src_ref=message.at[lax.rem(z + step, shards)],
-            dst_ref=arrived.at[step - 1],
-            send_sem=far_out.at[step - 1],
-            recv_sem=far_in.at[step - 1],
-            device_id={"atoms": lax.rem(z + step, shards)},
-            device_id_type=MESH,
-        )
-
-    for step in range(1, shards):
-        far_copy(step).start()
-    total = jnp.concatenate([acc_send[0:half_rows], acc_send[half_rows:]], axis=1)
-    total = total + message[z].astype(F32)
-    for step in range(1, shards):
-        far_copy(step).wait_recv()
-        total = total + arrived[step - 1].astype(F32)
-    tall[...] = total
+    lax.fori_loop(0, chunks - 1, work, 0)
+
+    prepare(chunks - 1)
+    for part, degrees in enumerate(PARTS):
+        first, last = degrees[0] ** 2, degrees[-1] ** 2 + 2 * degrees[-1] + 1
+        for i in range(wide // block):
+            rotate_chunk(grads, wig, rotated, pl.ds(i * block, block), degrees)
+        rows = slice(16 * first, 16 * last)
+
+        def finished(h, acc, hot):
+            return [
+                acc[half * half_rows + 16 * first : half * half_rows + 16 * last, :]
+                + dot_last(rotated[h, half, first:last].reshape(16 * (last - first), wide), hot[...])
+                for half in range(2)
+            ]
+
+        pair = finished(1, acc_recv, hot_recv)
+        for d in range(shards):
+            cut = slice(atoms * d, atoms * d + atoms)
+            message[d, rows] = jnp.concatenate([pair[0][:, cut], pair[1][:, cut]], axis=1).astype(BF16)
+        for step in STEPS[shards]:
+            far_copy(step, part).start()
+        tall[rows] = jnp.concatenate(finished(0, acc_send, hot_send), axis=1)
+    for part, degrees in enumerate(PARTS):
+        rows = slice(16 * degrees[0] ** 2, 16 * (degrees[-1] ** 2 + 2 * degrees[-1] + 1))
+        total = tall[rows] + message[z, rows].astype(F32)
+        for step in STEPS[shards]:
+            far_copy(step, part).wait_recv()
+            total = total + arrived[step - 1, rows].astype(F32)
+        tall[rows] = total
     for c in range(16):
         flat[:, 128 * c : 128 * c + 128] = tall[pl.ds(c, coefs, stride=16), :].astype(BF16)
     for i in range(8):
@@ -429,8 +450,9 @@
         return carry
 
     lax.fori_loop(0, chunks, finish, 0)
-    for step in range(1, shards):
-        far_copy(step).wait_send()
+    for part in range(len(PARTS)):
+        for step in STEPS[shards]:
+            far_copy(step, part).wait_send()
 
 
 def per_device(
@@ -529,8 +551,8 @@
             pltpu.SemaphoreType.DMA((8,)),
             pltpu.SemaphoreType.DMA((3, chunks)),
             pltpu.SemaphoreType.DMA((3, chunks)),
-            pltpu.SemaphoreType.DMA((shards - 1,)),
-            pltpu.SemaphoreType.DMA((shards - 1,)),
+            pltpu.SemaphoreType.DMA((shards - 1, len(PARTS))),
+            pltpu.SemaphoreType.DMA((shards - 1, len(PARTS))),
         ],
         compiler_params=pltpu.CompilerParams(
             collective_id=0, has_side_effects=True, vmem_limit_bytes=62 * 2**20

time: 64.2 us -> 64.2 us (level); the launches traced: 63.9 us -> 62.9 us
  Pallas kernels: 62.2 us -> 61.2 us
    pallas_call x1, Pallas kernels: 62.2 us -> 61.2 us  [per_device(): pl.pallas_call(functools.partial(fused_kernel, chunks), out_shape=jax.Sha...]
where the time goes in v3:
time: 64.2 us; the launch traced here: 62.9 us
  Pallas kernels  61.2 us (95%)
  local copies, waits for them, and re-layouts  1.77 us (3%)
    pallas_call x1, Pallas kernels, per_device(): pl.pallas_call(functools.partial(fused_kernel, chunks), out_shape=jax.Sha...  61.2 us
    unnamed x1, local copies, waits for them, and re-layouts  1.77 us

profile of v3, /device:TPU:9, one launch (start us, length us, event | category | flops | bytes accessed | tf_op | source)
XLA Modules:
  0.0 62.9 jit_solution(5952427149469257418)
XLA Ops:
  0.0 61.2 %shard_map.145 = bf16[49,32,64]{2,1,0:T(8,128)(2,1)} custom-call(bf16[29,16,1536]{2,1,0:T(8,128)(2,1)} %cot.1, bf16[235,1536]{1,0:T(8,128)(2,1)} %wigner_hbm.1, s32[12,128]{1,0:T(8,128)} %bitcast.16, s32[12,128]{1,0:T(8,128)} %bitcast.17, s32[12]{0:T(128)} %dests.1, s32[12]{0:T(128)} %lives.1, s32[12,32]{1,0:T(8,128)} %lists.1, ...), custom_call_target="tpu_custom_call" | custom-call | tf_op jit(solution)/shard_map/pallas_call | solution.py:521
  61.2 1.8 %copy.17 = bf16[49,32,64]{2,1,0:T(8,128)(2,1)} copy(bf16[49,32,64]{2,1,0:T(8,128)(2,1)} %shard_map.145) | data formatting | bytes 401408
